TPU v7x, 512 devices: a whole 4x8x8 slice. The times are simulated.
512 devices in a mesh: seq: 64 (over y, z), head: 8 (over x, core).
Axes of the slice: x: 4, y: 8, z: 8, core: 2. Of those that a mesh axis runs over, the one named last changes fastest.
Arguments:
- inputs: bfloat16 [8192, 16384], P('seq', 'head')
- b_proj: bfloat16 [8192, 1024], P('seq', 'head'), may hold values from -6 to 6
- c_proj: bfloat16 [8192, 1024], P('seq', 'head'), may hold values from -0.5 to 0.5
- log_decay: float32 [8192, 256], P('seq', 'head')
- skip: float32 [256], P('head'), may hold values from 0.5 to 2
- init_state: bfloat16 [256, 64, 128], P('head'), may hold values from -6 to 6
- norm_gain: float32 [16384], P('head'), may hold values from 0.5 to 1.5
Outputs:
- layer_output: bfloat16 [8192, 16384], P('seq', 'head')
All inputs are finite; a program needn't handle non-finite values.
Results may differ from a plain program's by a relative error of at most 0.0047.
Values sent between devices are 32-bit elements; how exact they have to be, the bound alone decides.
No kernel may reach another device: no remote copies, remote signals or barrier semaphores. Data moves between devices by JAX's collectives and lax.ppermute only.
A program may use at most 192 MiB of HBM per device.

v0:
```python
import jax
import jax.numpy as jnp
from jax import lax
from jax.sharding import PartitionSpec as P

RECURRENT_UNITS = 256
HEAD_DIM = 64
STATE = 128
BLOCK = 64


epsilon = 1e-05


def prefix(value, axis, join, neutral):
    count, mine = (lax.axis_size(axis), lax.axis_index(axis))
    pieces = jax.tree.map(lambda part: lax.all_gather(part, axis), value)
    subtotal = jax.tree.map(
        lambda part, zero: jnp.full_like(part, 0) + jnp.asarray(zero, part.dtype), value, neutral
    )

    def turn(position, subtotal):
        longer = join(subtotal, jax.tree.map(lambda part: part[position], pieces))
        return jax.tree.map(lambda new, old: jnp.where(position < mine, new, old), longer, subtotal)

    return lax.fori_loop(0, count - 1, turn, subtotal)


def carry_link(earlier, later):
    return (earlier[0] + later[0], jnp.exp(later[0])[:, None, None] * earlier[1] + later[1])


def local(inputs, b_proj, c_proj, log_decay, skip, init_state, norm_gain):
    tok_rows = inputs.shape[0]
    local_heads = log_decay.shape[1]
    local_groups = b_proj.shape[1] // STATE
    per_group = local_heads // local_groups
    blocks = tok_rows // BLOCK
    highest = lax.Precision.HIGHEST
    values_b = inputs.reshape(blocks, BLOCK, local_heads, HEAD_DIM)
    keys_b = b_proj.reshape(blocks, BLOCK, local_groups, STATE)
    query_c = c_proj.reshape(blocks, BLOCK, local_groups, STATE)
    cumulative = jnp.cumsum(log_decay.reshape(blocks, BLOCK, local_heads), axis=1)
    cumulative_h = jnp.transpose(cumulative, (0, 2, 1))
    block_decay = cumulative[:, -1, :]
    to_end = jnp.exp(cumulative[:, -1:, :] - cumulative)
    carried = (values_b.astype(jnp.float32) * to_end[:, :, :, None]).astype(jnp.bfloat16)
    weighted = carried.reshape(blocks, BLOCK, local_groups, per_group, HEAD_DIM)
    block_states = jnp.einsum(
        "kjgep,kjgn->kgepn", weighted, keys_b, preferred_element_type=jnp.float32
    )
    block_states = block_states.reshape(blocks, local_heads, HEAD_DIM, STATE)

    def advance(running, element):
        decay_log, fresh_state = element
        return (jnp.exp(decay_log)[:, None, None] * running + fresh_state, running)

    summary, entering = lax.scan(
        advance, jnp.zeros((local_heads, HEAD_DIM, STATE), jnp.float32), (block_decay, block_states)
    )
    total_decay = jnp.sum(block_decay, axis=0)
    prior_log = jnp.cumsum(block_decay, axis=0) - block_decay
    initial = init_state.astype(jnp.float32)
    prior_decay, prior_state = prefix(
        (total_decay, summary),
        "seq",
        carry_link,
        (jnp.zeros_like(total_decay), jnp.zeros_like(summary)),
    )
    arriving = prior_state + jnp.exp(prior_decay)[:, None, None] * initial
    scores = jnp.einsum("kign,kjgn->kgij", query_c, keys_b, preferred_element_type=jnp.float32)
    scores = jnp.repeat(scores, per_group, axis=1)
    rows_i = lax.broadcasted_iota(jnp.int32, (BLOCK, BLOCK), 0)
    cols_j = lax.broadcasted_iota(jnp.int32, (BLOCK, BLOCK), 1)
    causal = rows_i >= cols_j
    spread_log = cumulative_h[:, :, :, None] - cumulative_h[:, :, None, :]
    weights = (jnp.where(causal, jnp.exp(jnp.where(causal, spread_log, 0.0)), 0.0) * scores).astype(
        jnp.bfloat16
    )
    inside = jnp.einsum("khij,kjhp->kihp", weights, values_b, preferred_element_type=jnp.float32)
    query_f = query_c.astype(jnp.float32)
    local_grouped = entering.reshape(blocks, local_groups, per_group, HEAD_DIM, STATE)
    from_local = jnp.einsum("kign,kgepn->kigep", query_f, local_grouped, precision=highest)
    from_local = from_local.reshape(blocks, BLOCK, local_heads, HEAD_DIM)
    arrive_grouped = arriving.reshape(local_groups, per_group, HEAD_DIM, STATE)
    from_arrive = jnp.einsum("kign,gepn->kigep", query_f, arrive_grouped, precision=highest)
    from_arrive = (
        from_arrive.reshape(blocks, BLOCK, local_heads, HEAD_DIM)
        * jnp.exp(prior_log)[:, None, :, None]
    )
    outside = (from_local + from_arrive) * jnp.exp(cumulative)[:, :, :, None]
    result = inside + outside + skip[None, None, :, None] * values_b.astype(jnp.float32)
    flattened = result.reshape(tok_rows, local_heads * HEAD_DIM)
    squares = lax.psum(jnp.sum(flattened * flattened, axis=1), "head")
    factor = lax.rsqrt(squares / (RECURRENT_UNITS * HEAD_DIM) + epsilon)
    return (flattened * factor[:, None] * norm_gain[None, :]).astype(jnp.bfloat16)


def solution(mesh):
    in_specs = (
        P("seq", "head"),
        P("seq", "head"),
        P("seq", "head"),
        P("seq", "head"),
        P("head"),
        P("head", None, None),
        P("head"),
    )
    out_specs = P("seq", "head")
    return jax.shard_map(local, mesh=mesh, in_specs=in_specs, out_specs=out_specs, check_vma=False)
```

profile of v0, /device:TPU:1, one launch (start us, length us, event | category | flops | bytes accessed | tf_op | source)
XLA Modules:
  0.0 543.9 jit_solution(13628680549815332399)
XLA Ops:
  6.6 2.1 reshape.94
  8.6 2.0 copy.26
  11.0 1.6 fusion.9
  12.6 2.6 while.29
  18.7 129.0 %all-reduce = f32[2048]{0:T(1024)S(1)} all-reduce(f32[2048]{0:T(1024)S(1)} %dynamic-update-slice), channel_id=2, replica_groups=mesh['seq'=64,'head'=8] {'seq'}, use_global_device_ids=true, to_apply=%add | all-reduce | flops 2048 | bytes 16384
  148.0 3.5 fusion.8
  151.5 2.4 fusion.25
  153.9 265.5 %all-gather.4.cloned.1.call-done = f32[2048,64,128]{2,1,0:T(8,128)} async-done(((f32[32,64,128]{2,1,0:T(8,128)}), f32[2048,64,128]{2,1,0:T(8,128)}) %all-gather.4.cloned.1.call-update) | async-done | bytes 67108880 | tf_op jit(solution)/shard_map/all_gather | solution.py:17
  419.4 95.2 %while.30 = (s32[]{:T(128)}, f32[32]{0:T(128)S(1)}, f32[32,64,128]{2,1,0:T(8,128)S(1)}, s32[]{:T(128)}, f32[64,32]{1,0:T(8,128)S(1)}, /*index=5*/f32[64,32,64,128]{3,2,1,0:T(8,128)}, s32[]{:T(128)}, s32[]{:T(128)}) while((s32[]{:T(128)}, f32[32]{0:T(128)S(1)}, f32[32,64,128]{2,1,0:T(8,128)S(1)}, s32[]{:T(128)}, ...), condition=%wide.region_5.6_spmd.clone, body=%wide.region_4.5_spmd.clone.sunk | while | flops 1048676 | bytes 3146491 | solution.py:26
  419.5 1.6 fusion.36
  422.6 1.5 fusion.36
  424.1 1.5 fusion.36
  427.1 1.5 fusion.36
  428.6 1.5 fusion.36
  431.7 1.5 fusion.36
  433.2 1.5 fusion.36
  434.7 1.5 fusion.36
  436.2 1.5 fusion.36
  437.7 1.5 fusion.36
  439.2 1.5 fusion.36
  440.7 1.5 fusion.36
  442.2 1.5 fusion.36
  443.7 1.5 fusion.36
  445.3 1.5 fusion.36
  446.8 1.5 fusion.36
  448.3 1.5 fusion.36
  451.3 1.5 fusion.36
  452.8 1.5 fusion.36
  455.8 1.5 fusion.36
  457.3 1.5 fusion.36
  460.4 1.5 fusion.36
  461.9 1.5 fusion.36
  463.4 1.5 fusion.36
  464.9 1.5 fusion.36
  466.4 1.5 fusion.36
  467.9 1.5 fusion.36
  469.4 1.5 fusion.36
  470.9 1.5 fusion.36
  472.4 1.5 fusion.36
  474.0 1.5 fusion.36
  475.5 1.5 fusion.36
  477.0 1.5 fusion.36
  480.0 1.5 fusion.36
  481.5 1.5 fusion.36
  484.5 1.5 fusion.36
  514.7 5.0 multiply_reduce_fusion
  519.8 3.1 copy.31
  523.6 12.4 %psum.7 = f32[128]{0:T(128)S(1)} all-reduce(f32[128]{0:T(128)S(1)} %reduce_sum.22), channel_id=1, replica_groups=mesh['seq'=64,'head'=8] {'head'}, use_global_device_ids=true, to_apply=%region_8.9 | all-reduce | flops 128 | bytes 1024 | tf_op jit(solution)/shard_map/psum | solution.py:94
  (140 shorter events, 48.3 us)
Async XLA Ops:
  6.5 141.4 %copy-start = (bf16[128,128]{1,0:T(8,128)(2,1)S(1)}, bf16[128,128]{1,0:T(8,128)(2,1)}, u32[]{:S(2)}) copy-start(bf16[128,128]{1,0:T(8,128)(2,1)} %param.13) | copy-start | bytes 98308
  6.5 4.1 copy-start.6
  6.5 412.9 %all-gather.4.cloned.1.call-start = ((), (), s32[]{:S(2)}) async-start(), calls=%async_computation | async-start | bytes 68157440 | tf_op jit(solution)/shard_map/all_gather | solution.py:17
  6.5 4.4 copy-start.5
  15.2 1.0 copy-start.1
  148.0 3.5 copy-start.3
  419.4 95.3 %copy-start.2 = (bf16[2,64,32,64]{1,3,2,0:T(8,128)(2,1)S(1)}, bf16[2,64,32,64]{1,3,2,0:T(8,128)(2,1)}, u32[]{:S(2)}) copy-start(bf16[2,64,32,64]{1,3,2,0:T(8,128)(2,1)} %copy.26) | copy-start | bytes 1572868
  419.4 95.3 %copy-start.4 = (bf16[32,64,128]{2,1,0:T(8,128)(2,1)S(1)}, bf16[32,64,128]{2,1,0:T(8,128)(2,1)}, u32[]{:S(2)}) copy-start(bf16[32,64,128]{2,1,0:T(8,128)(2,1)} %param.16) | copy-start | bytes 1572868
  419.4 95.3 %copy-start.8 = (f32[32]{0:T(128)S(1)}, f32[32]{0:T(128)}, u32[]{:S(2)}) copy-start(f32[32]{0:T(128)} %param.15) | copy-start | bytes 388
  522.9 13.2 %copy-start.7 = (f32[2048]{0:T(1024)S(1)}, f32[2048]{0:T(1024)}, u32[]{:S(2)}) copy-start(f32[2048]{0:T(1024)} %param.17) | copy-start | bytes 24580
Sparse Core Ops, SparseCore 0:
  16.4 403.0 all-gather.3
where the time goes:
time: 547 us; the launch traced here: 544 us
  waiting for transfers between devices  266 us (49%)
  blocking collectives  141 us (26%)
  other arithmetic  97.2 us (18%)
  between operations  14.2 us (3%)
  matrix products  12.7 us (2%)
  local copies, waits for them, and re-layouts  11 us (2%)
    all_gather x1, waiting for transfers between devices, prefix(): pieces = jax.tree.map(lambda part: lax.all_gather(part, axis), value)  266 us
    unnamed x1, blocking collectives  129 us
    select_n x63, other arithmetic, turn(): jnp.where(position < mine, new, old)  92.4 us
    psum x1, blocking collectives, local(): squares = lax.psum(jnp.sum(flattened * flattened, axis=1), 'head')  12.4 us
  transfers between devices with their start and end apart: 1, of which 1 were waited for; matrix products, arithmetic and copies ran while one was open for 1% of the time, Pallas kernels for 0%

commit v1 on v0

v1 whole, which is shorter than its diff:
```python
import jax
import jax.numpy as jnp
from jax import lax
from jax.experimental import pallas as pl
from jax.experimental.pallas import tpu as pltpu
from jax.sharding import PartitionSpec as P

RECURRENT_UNITS = 256
HEAD_DIM = 64
STATE = 128
BLOCK = 64
TOK = 128
PAIRS = 16
SEQ = 64
CUT = 4
ROWS = STATE // CUT
SENT = ROWS + 1
EPSILON = 1e-05
INTERPRET = False

F32, BF16 = jnp.float32, jnp.bfloat16
HIGHEST = lax.Precision.HIGHEST


def iotas(shape):
    return lax.broadcasted_iota(jnp.int32, shape, 0), lax.broadcasted_iota(jnp.int32, shape, 1)


def ones_where(condition):
    return jnp.where(condition, 1.0, 0.0).astype(F32)


def by_head(values, pair):
    rows = values.shape[0]
    lane = lax.broadcasted_iota(jnp.int32, (rows, 128), 1)
    left = jnp.broadcast_to(values[:, 2 * pair : 2 * pair + 1], (rows, 128))
    right = jnp.broadcast_to(values[:, 2 * pair + 1 : 2 * pair + 2], (rows, 128))
    return jnp.where(lane < HEAD_DIM, left, right)


def summed(decay_ref, mask):
    return jnp.dot(decay_ref[...], ones_where(mask), precision=HIGHEST, preferred_element_type=F32)


def states_kernel(x_ref, b_ref, decay_ref, out_ref):
    row, col = iotas((TOK, TOK))
    after = summed(decay_ref, row > col).T
    to_end = jnp.exp(after)
    total = summed(decay_ref, row >= 0).T[0:1]
    keys = b_ref[...].astype(F32).T.astype(BF16)
    for pair in range(PAIRS):
        lanes = slice(128 * pair, 128 * pair + 128)
        carried = (x_ref[:, lanes].astype(F32) * by_head(to_end, pair)).astype(BF16)
        state = jnp.dot(keys, carried, preferred_element_type=F32)
        total_row = by_head(total, pair)
        for cut in range(CUT):
            base = SENT * (CUT * pair + cut)
            out_ref[base : base + ROWS, :] = state[ROWS * cut : ROWS * cut + ROWS]
            out_ref[base + ROWS : base + SENT, :] = total_row


def scan_kernel(states_ref, init_ref, out_ref, first):
    me = lax.axis_index("seq")
    pair, cut = me // CUT, me % CUT
    start = init_ref[pl.ds(2 * pair, 2)].astype(F32).reshape(2 * HEAD_DIM, STATE)
    first[...] = start.T
    running = first[pl.ds(pl.multiple_of(ROWS * cut, ROWS), ROWS), :]
    for device in range(SEQ):
        base = SENT * device
        out_ref[ROWS * device : ROWS * device + ROWS, :] = running
        factor = jnp.exp(states_ref[base + ROWS : base + SENT, :])
        running = factor * running + states_ref[base : base + ROWS, :]


def output_kernel(x_ref, b_ref, c_ref, decay_ref, skip_ref, entry_ref, y_ref, squares_ref):
    row, col = iotas((TOK, TOK))
    same = (row // BLOCK) == (col // BLOCK)
    in_block_t = summed(decay_ref, same & (row <= col))
    second_t = jnp.where(col[:32] < BLOCK, -summed(decay_ref, (row > col) & (row < BLOCK)), in_block_t)
    in_block = in_block_t.T
    grown = jnp.exp(summed(decay_ref, row <= col).T)
    query, keys = c_ref[...], b_ref[...]
    scores = lax.dot_general(query, keys, (((1,), (1,)), ((), ())), preferred_element_type=F32)
    twice = jnp.concatenate([query, query], axis=1)
    row_h, col_h = iotas((BLOCK, TOK))
    left = col_h < HEAD_DIM
    top_mask = (col_h % BLOCK) <= row_h
    low_mask = col_h <= row_h + BLOCK
    top_scores = scores[:BLOCK, :BLOCK]
    top_scores = jnp.concatenate([top_scores, top_scores], axis=1)
    low_scores = scores[BLOCK:]
    skip = skip_ref[...]
    total = jnp.zeros((TOK, 128), F32)
    half_lane = lax.broadcasted_iota(jnp.int32, (TOK, 128), 1) < HEAD_DIM
    zero = jnp.zeros((TOK, 128), BF16)
    for pair in range(PAIRS):
        lanes = slice(128 * pair, 128 * pair + 128)
        h0, h1 = 2 * pair, 2 * pair + 1
        x = x_ref[:, lanes]
        x0 = jnp.where(half_lane, x, zero)
        x1 = jnp.where(half_lane, zero, x)
        top_row = jnp.concatenate([in_block_t[h0 : h0 + 1, :BLOCK], in_block_t[h1 : h1 + 1, :BLOCK]], axis=1)
        top = by_head(in_block[:BLOCK], pair) - top_row
        top = (jnp.exp(jnp.where(top_mask, top, -1e30)) * top_scores).astype(BF16)
        low = []
        for h in (h0, h1):
            spread = in_block[BLOCK:, h : h + 1] - second_t[h : h + 1, :]
            low.append((jnp.exp(jnp.where(low_mask, spread, -1e30)) * low_scores).astype(BF16))
        top_values = jnp.concatenate([x0[:BLOCK], x1[:BLOCK]], axis=0)
        inside_top = jnp.dot(top, top_values, preferred_element_type=F32)
        inside_low = jnp.dot(
            jnp.concatenate(low, axis=1), jnp.concatenate([x0, x1], axis=0), preferred_element_type=F32
        )
        inside = jnp.concatenate([inside_top, inside_low], axis=0)
        entry = entry_ref[128 * pair : 128 * pair + 128, :]
        high = entry.astype(BF16)
        rest = (entry - high.astype(F32)).astype(BF16)
        outside = jnp.dot(twice, jnp.concatenate([high, rest], axis=0), preferred_element_type=F32)
        y = inside + outside * by_head(grown, pair) + by_head(skip, pair) * x.astype(F32)
        y_ref[:, lanes] = y
        total = total + y * y
    squares_ref[...] = jnp.sum(total.T, axis=0, keepdims=True)


def norm_kernel(y_ref, squares_ref, gain_ref, out_ref):
    mean = jnp.sum(squares_ref[...], axis=0, keepdims=True) / (RECURRENT_UNITS * HEAD_DIM)
    factor = jnp.broadcast_to(lax.rsqrt(mean + EPSILON), (TOK, TOK)).T
    for pair in range(PAIRS):
        lanes = slice(128 * pair, 128 * pair + 128)
        out_ref[:, lanes] = (y_ref[:, lanes] * factor * gain_ref[:, lanes]).astype(BF16)


def call(kernel, outs, *args, scratch=()):
    return pl.pallas_call(
        kernel,
        out_shape=outs,
        scratch_shapes=scratch,
        interpret=INTERPRET,
        compiler_params=pltpu.CompilerParams(vmem_limit_bytes=32 * 1024 * 1024),
    )(*args)


def local(inputs, b_proj, c_proj, log_decay, skip, init_state, norm_gain):
    shape = jax.ShapeDtypeStruct
    decay = log_decay.T
    states = call(states_kernel, shape((SEQ * SENT, 128), F32), inputs, b_proj, decay)
    states = lax.all_to_all(states.reshape(SEQ, SENT, 1, 128), "seq", 0, 0, tiled=True)
    entries = call(
        scan_kernel,
        shape((SEQ * ROWS, 128), F32),
        states.reshape(SEQ * SENT, 128),
        init_state,
        scratch=[pltpu.VMEM((STATE, 128), F32)],
    )
    entries = lax.all_to_all(entries.reshape(SEQ, ROWS, 128), "seq", 0, 0, tiled=True)
    y, squares = call(
        output_kernel,
        (shape((TOK, PAIRS * 128), F32), shape((1, TOK), F32)),
        inputs,
        b_proj,
        c_proj,
        decay,
        skip.reshape(1, -1),
        entries.reshape(SEQ * ROWS, 128),
    )
    squares = lax.all_gather(squares, "head", axis=0, tiled=True)
    return call(norm_kernel, shape((TOK, PAIRS * 128), BF16), y, squares, norm_gain.reshape(1, -1))


def solution(mesh):
    in_specs = (
        P("seq", "head"),
        P("seq", "head"),
        P("seq", "head"),
        P("seq", "head"),
        P("head"),
        P("head", None, None),
        P("head"),
    )
    out_specs = P("seq", "head")
    return jax.shard_map(local, mesh=mesh, in_specs=in_specs, out_specs=out_specs, check_vma=False)
```

time: 547 us -> 102 us (0.19)
  waiting for transfers between devices: 266 us -> 0 us
  other arithmetic: 97.2 us -> 0 us
  blocking collectives: 141 us -> 94.3 us
  between operations: 14.2 us -> 0.04 us
  matrix products: 12.7 us -> 0 us
  local copies, waits for them, and re-layouts: 11 us -> 2.54 us
    all_gather x1 -> x0, waiting for transfers between devices: 266 us -> none  [prefix(): pieces = jax.tree.map(lambda part: lax.all_gather(part, axis), value)]
    unnamed x1 -> x0, blocking collectives: 129 us -> none
    select_n x63 -> x0, other arithmetic: 92.4 us -> none  [turn(): jnp.where(position < mine, new, old)]
    all_to_all x0 -> x2, blocking collectives: none -> 80 us  [the longest x1 44.4 us: local(): lax.all_to_all(states.reshape(SEQ, SENT, 1, 128), 'seq', 0, 0, tiled=True)]
    all_gather x0 -> x1, blocking collectives: none -> 14.3 us  [local(): squares = lax.all_gather(squares, 'head', axis=0, tiled=True)]
    dot_general x5 -> x0, matrix products: 12.7 us -> none  [the longest x1 5.02 us: local(): jnp.einsum('kign,gepn->kigep', query_f, arrive_grouped, precision=highest)]
    psum x1 -> x0, blocking collectives: 12.4 us -> none  [local(): squares = lax.psum(jnp.sum(flattened * flattened, axis=1), 'head')]
  transfers between devices with their start and end apart: 1 -> 0, of which waited for: 1 -> 0; matrix products, arithmetic and copies ran while one was open for 1% -> 0% of each run, Pallas kernels for 0% -> 0%
where the time goes in v1:
time: 102 us
  blocking collectives  94.3 us (92%)
  Pallas kernels  4.73 us (5%)
  local copies, waits for them, and re-layouts  2.54 us (2%)
    all_to_all x1, blocking collectives, local(): lax.all_to_all(states.reshape(SEQ, SENT, 1, 128), 'seq', 0, 0, tiled=True)  44.4 us
    all_to_all x1, blocking collectives, local(): lax.all_to_all(entries.reshape(SEQ, ROWS, 128), 'seq', 0, 0, tiled=True)  35.6 us
    all_gather x1, blocking collectives, local(): squares = lax.all_gather(squares, 'head', axis=0, tiled=True)  14.3 us
    pallas_call x4, Pallas kernels, call(): pl.pallas_call(kernel, out_shape=outs, scratch_shapes=scratch, interpret=...  4.73 us
    unnamed x14, local copies, waits for them, and re-layouts  2.54 us

profile of v1, /device:TPU:1, one launch (start us, length us, event | category | flops | bytes accessed | tf_op | source)
XLA Modules:
  0.0 101.6 jit_solution(14664697690488298133)
XLA Ops:
  0.0 0.0 copy-start
  0.0 1.0 %copy-done = bf16[128,2048]{1,0:T(8,128)(2,1)S(1)} copy-done((bf16[128,2048]{1,0:T(8,128)(2,1)S(1)}, bf16[128,2048]{1,0:T(8,128)(2,1)}, u32[]{:S(2)}) %copy-start) | copy-done | bytes 524312
  1.0 0.0 copy-start.2
  1.0 0.8 copy-done.2
  1.8 0.0 copy-start.3
  1.8 0.7 copy-done.3
  2.5 1.3 %shard_map.73 = f32[2112,128]{1,0:T(8,128)S(1)} custom-call(bf16[128,2048]{1,0:T(8,128)(2,1)S(1)} %copy-done, bf16[128,128]{1,0:T(8,128)(2,1)S(1)} %copy-done.2, f32[32,128]{1,0:T(8,128)S(1)} %bitcast.13), custom_call_target="tpu_custom_call" | custom-call | tf_op jit(solution)/shard_map/pallas_call | solution.py:134
  3.9 0.0 copy-start.1
  3.9 44.4 %all_to_all.10 = f32[64,33,1,128]{3,2,1,0:T(1,128)S(1)} all-to-all(f32[64,33,1,128]{3,2,1,0:T(1,128)S(1)} %bitcast.9), channel_id=1, replica_groups=mesh['seq'=64,'head'=8] {'seq'}, dimensions={0} | all-to-all | bytes 2162688 | tf_op jit(solution)/shard_map/all_to_all | solution.py:147
  48.3 0.0 copy-done.1
  48.3 0.2 shard_map.74
  48.6 0.0 copy-start.4
  48.6 0.0 copy-start.6
  48.6 35.6 %all_to_all.11 = f32[64,32,128]{2,1,0:T(8,128)S(1)} all-to-all(f32[64,32,128]{2,1,0:T(8,128)S(1)} %bitcast.12), channel_id=1, replica_groups=mesh['seq'=64,'head'=8] {'seq'}, dimensions={0} | all-to-all | bytes 2097152 | tf_op jit(solution)/shard_map/all_to_all | solution.py:155
  84.1 0.0 copy-start.5
  84.2 0.0 copy-done.4
  84.2 0.0 copy-done.6
  84.2 2.1 %shard_map.75 = (f32[128,2048]{1,0:T(8,128)S(1)}, f32[1,128]{1,0:T(1,128)S(1)}) custom-call(bf16[128,2048]{1,0:T(8,128)(2,1)S(1)} %copy-done, bf16[128,128]{1,0:T(8,128)(2,1)S(1)} %copy-done.2, bf16[128,128]{1,0:T(8,128)(2,1)S(1)} %copy-done.4, f32[32,128]{1,0:T(8,128)S(1)} %bitcast.14, f32[1,32]{1,0:T(1,128)S(1)} %bitcast.17, f32[2048,128]{1,0:T(8,128)S(1)} %bitcast.11), custom_call_target="tpu_custom_call" | custom-call | tf_op jit(solution)/shard_map/pallas_call | solution.py:134
  86.3 14.3 %all-gather = f32[8,1,128]{2,1,0:T(1,128)S(1)} all-gather(f32[1,1,128]{2,1,0:T(1,128)S(1)} %bitcast.18), channel_id=1, replica_groups=mesh['seq'=64,'head'=8] {'head'}, dimensions={0}, use_global_device_ids=true | all-gather | bytes 4608 | tf_op jit(solution)/shard_map/all_gather | solution.py:166
  100.6 0.0 copy-done.5
  100.6 1.0 shard_map.76
Async XLA Ops:
  0.0 1.0 %copy-start = (bf16[128,2048]{1,0:T(8,128)(2,1)S(1)}, bf16[128,2048]{1,0:T(8,128)(2,1)}, u32[]{:S(2)}) copy-start(bf16[128,2048]{1,0:T(8,128)(2,1)} %x_ref.3) | copy-start | bytes 1572868
  1.0 0.8 copy-start.2
  1.8 0.7 copy-start.3
  3.9 44.4 %copy-start.1 = (bf16[32,64,128]{2,1,0:T(8,128)(2,1)S(1)}, bf16[32,64,128]{2,1,0:T(8,128)(2,1)}, u32[]{:S(2)}) copy-start(bf16[32,64,128]{2,1,0:T(8,128)(2,1)} %init_ref.1) | copy-start | bytes 1572868
  48.6 35.6 %copy-start.4 = (bf16[128,128]{1,0:T(8,128)(2,1)S(1)}, bf16[128,128]{1,0:T(8,128)(2,1)}, u32[]{:S(2)}) copy-start(bf16[128,128]{1,0:T(8,128)(2,1)} %c_ref.1) | copy-start | bytes 98308
  48.6 35.6 %copy-start.6 = (f32[32]{0:T(128)S(1)}, f32[32]{0:T(128)}, u32[]{:S(2)}) copy-start(f32[32]{0:T(128)} %param.11) | copy-start | bytes 388
  84.1 16.5 %copy-start.5 = (f32[2048]{0:T(1024)S(1)}, f32[2048]{0:T(1024)}, u32[]{:S(2)}) copy-start(f32[2048]{0:T(1024)} %param.13) | copy-start | bytes 24580

commit v2 on v1

--- a/solution.py
+++ b/solution.py
@@ -15,6 +15,10 @@
 CUT = 4
 ROWS = STATE // CUT
 SENT = ROWS + 1
+PARTS = 2
+WIDTH = PAIRS * 128 // PARTS
+FIRST = [8 * ((SEQ - 1 - k) % 8) + (SEQ - 1 - k) // 8 for k in range(SEQ)]
+SECOND = [SEQ - 1 - k for k in range(SEQ)]
 EPSILON = 1e-05
 INTERPRET = False
 
@@ -42,13 +46,28 @@
     return jnp.dot(decay_ref[...], ones_where(mask), precision=HIGHEST, preferred_element_type=F32)
 
 
-def states_kernel(x_ref, b_ref, decay_ref, out_ref):
+def states_kernel(x_hbm, b_hbm, decay_hbm, out_hbm, x_ref, b_ref, decay_ref, out_ref, sems, out_sems):
+    copies = [
+        pltpu.make_async_copy(decay_hbm, decay_ref, sems.at[0]),
+        pltpu.make_async_copy(b_hbm, b_ref, sems.at[1]),
+    ]
+    for part in range(PARTS):
+        lanes = pl.ds(WIDTH * part, WIDTH)
+        copies.append(
+            pltpu.make_async_copy(x_hbm.at[:, lanes], x_ref.at[:, lanes], sems.at[2 + part])
+        )
+    for copy in copies:
+        copy.start()
     row, col = iotas((TOK, TOK))
+    copies[0].wait()
     after = summed(decay_ref, row > col).T
     to_end = jnp.exp(after)
-    total = summed(decay_ref, row >= 0).T[0:1]
+    total = after[0:1] + decay_ref[...].T[0:1]
+    copies[1].wait()
     keys = b_ref[...].astype(F32).T.astype(BF16)
     for pair in range(PAIRS):
+        if pair % (PAIRS // PARTS) == 0:
+            copies[2 + pair // (PAIRS // PARTS)].wait()
         lanes = slice(128 * pair, 128 * pair + 128)
         carried = (x_ref[:, lanes].astype(F32) * by_head(to_end, pair)).astype(BF16)
         state = jnp.dot(keys, carried, preferred_element_type=F32)
@@ -57,22 +76,35 @@
             base = SENT * (CUT * pair + cut)
             out_ref[base : base + ROWS, :] = state[ROWS * cut : ROWS * cut + ROWS]
             out_ref[base + ROWS : base + SENT, :] = total_row
-
-
-def scan_kernel(states_ref, init_ref, out_ref, first):
-    me = lax.axis_index("seq")
-    pair, cut = me // CUT, me % CUT
-    start = init_ref[pl.ds(2 * pair, 2)].astype(F32).reshape(2 * HEAD_DIM, STATE)
-    first[...] = start.T
-    running = first[pl.ds(pl.multiple_of(ROWS * cut, ROWS), ROWS), :]
+        if (pair + 1) % (PAIRS // PARTS) == 0:
+            part = pair // (PAIRS // PARTS)
+            rows = pl.ds(SEQ * SENT // PARTS * part, SEQ * SENT // PARTS)
+            copies.append(
+                pltpu.make_async_copy(out_ref.at[rows], out_hbm.at[rows], out_sems.at[part])
+            )
+            copies[-1].start()
+    for copy in copies[2 + PARTS :]:
+        copy.wait()
+
+
+def scan_kernel(states_ref, first_ref, out_ref):
+    running = first_ref[...]
     for device in range(SEQ):
-        base = SENT * device
-        out_ref[ROWS * device : ROWS * device + ROWS, :] = running
+        base = SENT * FIRST.index(device)
+        place = ROWS * SECOND.index(device)
+        out_ref[place : place + ROWS, :] = running
         factor = jnp.exp(states_ref[base + ROWS : base + SENT, :])
         running = factor * running + states_ref[base : base + ROWS, :]
 
 
-def output_kernel(x_ref, b_ref, c_ref, decay_ref, skip_ref, entry_ref, y_ref, squares_ref):
+def inside_kernel(
+    x_ref, b_ref, c_ref, decay_ref, skip_ref, init_ref, inside_ref, grown_ref, first_ref, slice_ref
+):
+    me = lax.axis_index("seq")
+    place = SEQ - 1 - (8 * (me % 8) + me // 8)
+    start = init_ref[pl.ds(2 * (place // CUT), 2)].astype(F32).reshape(2 * HEAD_DIM, STATE)
+    slice_ref[...] = start.T
+    first_ref[...] = slice_ref[pl.ds(pl.multiple_of(ROWS * (place % CUT), ROWS), ROWS), :]
     row, col = iotas((TOK, TOK))
     same = (row // BLOCK) == (col // BLOCK)
     in_block_t = summed(decay_ref, same & (row <= col))
@@ -81,7 +113,6 @@
     grown = jnp.exp(summed(decay_ref, row <= col).T)
     query, keys = c_ref[...], b_ref[...]
     scores = lax.dot_general(query, keys, (((1,), (1,)), ((), ())), preferred_element_type=F32)
-    twice = jnp.concatenate([query, query], axis=1)
     row_h, col_h = iotas((BLOCK, TOK))
     left = col_h < HEAD_DIM
     top_mask = (col_h % BLOCK) <= row_h
@@ -90,7 +121,6 @@
     top_scores = jnp.concatenate([top_scores, top_scores], axis=1)
     low_scores = scores[BLOCK:]
     skip = skip_ref[...]
-    total = jnp.zeros((TOK, 128), F32)
     half_lane = lax.broadcasted_iota(jnp.int32, (TOK, 128), 1) < HEAD_DIM
     zero = jnp.zeros((TOK, 128), BF16)
     for pair in range(PAIRS):
@@ -112,59 +142,119 @@
             jnp.concatenate(low, axis=1), jnp.concatenate([x0, x1], axis=0), preferred_element_type=F32
         )
         inside = jnp.concatenate([inside_top, inside_low], axis=0)
-        entry = entry_ref[128 * pair : 128 * pair + 128, :]
+        grown_ref[:, lanes] = by_head(grown, pair)
+        inside_ref[:, lanes] = inside + by_head(skip, pair) * x.astype(F32)
+
+
+def output_kernel(c_ref, inside_ref, grown_ref, entry_ref, y_ref, squares_ref):
+    query = c_ref[...]
+    twice = jnp.concatenate([query, query], axis=1)
+    total = jnp.zeros((TOK, 128), F32)
+    for pair in range(PAIRS):
+        lanes = slice(128 * pair, 128 * pair + 128)
+        places = [ROWS * SECOND.index(FIRST[CUT * pair + cut]) for cut in range(CUT)]
+        entry = jnp.concatenate([entry_ref[place : place + ROWS, :] for place in places], axis=0)
         high = entry.astype(BF16)
         rest = (entry - high.astype(F32)).astype(BF16)
         outside = jnp.dot(twice, jnp.concatenate([high, rest], axis=0), preferred_element_type=F32)
-        y = inside + outside * by_head(grown, pair) + by_head(skip, pair) * x.astype(F32)
+        y = inside_ref[:, lanes] + outside * grown_ref[:, lanes]
         y_ref[:, lanes] = y
         total = total + y * y
     squares_ref[...] = jnp.sum(total.T, axis=0, keepdims=True)
 
 
-def norm_kernel(y_ref, squares_ref, gain_ref, out_ref):
+def norm_kernel(y_ref, squares_ref, gain_ref, out_hbm, out_ref, sems):
     mean = jnp.sum(squares_ref[...], axis=0, keepdims=True) / (RECURRENT_UNITS * HEAD_DIM)
+    copies = []
     factor = jnp.broadcast_to(lax.rsqrt(mean + EPSILON), (TOK, TOK)).T
     for pair in range(PAIRS):
         lanes = slice(128 * pair, 128 * pair + 128)
         out_ref[:, lanes] = (y_ref[:, lanes] * factor * gain_ref[:, lanes]).astype(BF16)
-
-
-def call(kernel, outs, *args, scratch=()):
-    return pl.pallas_call(
-        kernel,
-        out_shape=outs,
-        scratch_shapes=scratch,
-        interpret=INTERPRET,
-        compiler_params=pltpu.CompilerParams(vmem_limit_bytes=32 * 1024 * 1024),
-    )(*args)
+        if (pair + 1) % (PAIRS // PARTS) == 0:
+            part = pair // (PAIRS // PARTS)
+            lanes = pl.ds(WIDTH * part, WIDTH)
+            copies.append(
+                pltpu.make_async_copy(out_ref.at[:, lanes], out_hbm.at[:, lanes], sems.at[part])
+            )
+            copies[-1].start()
+    for copy in copies:
+        copy.wait()
+
+
+def call(kernel, outs, *args, **more):
+    params = pltpu.CompilerParams(vmem_limit_bytes=32 * 1024 * 1024)
+    return pl.pallas_call(kernel, out_shape=outs, interpret=INTERPRET, compiler_params=params, **more)(*args)
+
+
+def in_hbm(value):
+    return value if INTERPRET else pltpu.with_memory_space_constraint(value, pltpu.HBM)
+
+
+def exchange(slices, order):
+    return lax.all_to_all(slices, "seq", 0, 0, tiled=True, axis_index_groups=[order])
 
 
 def local(inputs, b_proj, c_proj, log_decay, skip, init_state, norm_gain):
     shape = jax.ShapeDtypeStruct
+    whole = shape((TOK, PAIRS * 128), F32)
+    anywhere = pl.BlockSpec(memory_space=pl.ANY)
     decay = log_decay.T
-    states = call(states_kernel, shape((SEQ * SENT, 128), F32), inputs, b_proj, decay)
-    states = lax.all_to_all(states.reshape(SEQ, SENT, 1, 128), "seq", 0, 0, tiled=True)
-    entries = call(
-        scan_kernel,
-        shape((SEQ * ROWS, 128), F32),
-        states.reshape(SEQ * SENT, 128),
-        init_state,
-        scratch=[pltpu.VMEM((STATE, 128), F32)],
-    )
-    entries = lax.all_to_all(entries.reshape(SEQ, ROWS, 128), "seq", 0, 0, tiled=True)
-    y, squares = call(
-        output_kernel,
-        (shape((TOK, PAIRS * 128), F32), shape((1, TOK), F32)),
+    states = call(
+        states_kernel,
+        shape((SEQ * SENT, 128), F32),
+        in_hbm(inputs),
+        in_hbm(b_proj),
+        in_hbm(decay),
+        in_specs=[anywhere] * 3,
+        out_specs=anywhere,
+        scratch_shapes=[
+            pltpu.VMEM(inputs.shape, BF16),
+            pltpu.VMEM(b_proj.shape, BF16),
+            pltpu.VMEM(decay.shape, F32),
+            pltpu.VMEM((SEQ * SENT, 128), F32),
+            pltpu.SemaphoreType.DMA((2 + PARTS,)),
+            pltpu.SemaphoreType.DMA((PARTS,)),
+        ],
+    )
+    states = exchange(states.reshape(SEQ, SENT, 1, 128), FIRST)
+    inside, grown, first = call(
+        inside_kernel,
+        (whole, whole, shape((ROWS, 128), F32)),
         inputs,
         b_proj,
         c_proj,
         decay,
         skip.reshape(1, -1),
+        init_state,
+        scratch_shapes=[pltpu.VMEM((STATE, 128), F32)],
+        cost_estimate=pl.CostEstimate(flops=1 << 31, bytes_accessed=1 << 24, transcendentals=1 << 20),
+    )
+    entries = call(
+        scan_kernel,
+        shape((SEQ * ROWS, 128), F32),
+        states.reshape(SEQ * SENT, 128),
+        first,
+    )
+    entries = exchange(entries.reshape(SEQ, ROWS, 128), SECOND)
+    y, squares = call(
+        output_kernel,
+        (whole, shape((1, TOK), F32)),
+        c_proj,
+        inside,
+        grown,
         entries.reshape(SEQ * ROWS, 128),
     )
-    squares = lax.all_gather(squares, "head", axis=0, tiled=True)
-    return call(norm_kernel, shape((TOK, PAIRS * 128), BF16), y, squares, norm_gain.reshape(1, -1))
+    order = list(range(lax.axis_size("head")))[::-1]
+    squares = lax.all_gather(squares, "head", axis=0, tiled=True, axis_index_groups=[order])
+    return call(
+        norm_kernel,
+        shape((TOK, PAIRS * 128), BF16),
+        y,
+        squares,
+        norm_gain.reshape(1, -1),
+        out_specs=anywhere,
+        scratch_shapes=[pltpu.VMEM((TOK, PAIRS * 128), BF16), pltpu.SemaphoreType.DMA((PARTS,))],
+    )
 
 
 def solution(mesh):

time: 102 us -> 94.7 us (0.928)
  blocking collectives: 94.3 us -> 45.6 us
  waiting for transfers between devices: 0 us -> 22.4 us
  starting transfers between devices: 0 us -> 17.4 us
  Pallas kernels: 4.73 us -> 6.69 us
    all_to_all x2 -> x1, blocking collectives: 80 us -> 31.7 us  [exchange(): lax.all_to_all(slices, 'seq', 0, 0, tiled=True, axis_index_groups=[order])]
    all_to_all x0 -> x1, waiting for transfers between devices: none -> 22.4 us  [exchange(): lax.all_to_all(slices, 'seq', 0, 0, tiled=True, axis_index_groups=[order])]
    all_to_all x0 -> x1, starting transfers between devices: none -> 17.4 us  [exchange(): lax.all_to_all(slices, 'seq', 0, 0, tiled=True, axis_index_groups=[order])]
    pallas_call x4 -> x5, Pallas kernels: 4.73 us -> 6.69 us  [call(): pl.pallas_call(kernel, out_shape=outs, interpret=INTERPRET, compiler_para...]
  transfers between devices with their start and end apart: 0 -> 1, of which waited for: 0 -> 1; matrix products, arithmetic and copies ran while one was open for 0% -> 0% of each run, Pallas kernels for 0% -> 2%
where the time goes in v2:
time: 94.7 us; the launch traced here: 94.3 us
  blocking collectives  45.6 us (48%)
  waiting for transfers between devices  22.4 us (24%)
  starting transfers between devices  17.4 us (18%)
  Pallas kernels  6.69 us (7%)
  local copies, waits for them, and re-layouts  2.11 us (2%)
    all_to_all x1, blocking collectives, exchange(): lax.all_to_all(slices, 'seq', 0, 0, tiled=True, axis_index_groups=[order])  31.7 us
    all_to_all x1, waiting for transfers between devices, exchange(): lax.all_to_all(slices, 'seq', 0, 0, tiled=True, axis_index_groups=[order])  22.4 us
    all_to_all x1, starting transfers between devices, exchange(): lax.all_to_all(slices, 'seq', 0, 0, tiled=True, axis_index_groups=[order])  17.4 us
    all_gather x1, blocking collectives, local(): lax.all_gather(squares, 'head', axis=0, tiled=True, axis_index_groups=[or...  13.9 us
    pallas_call x5, Pallas kernels, call(): pl.pallas_call(kernel, out_shape=outs, interpret=INTERPRET, compiler_para...  6.69 us
    unnamed x14, local copies, waits for them, and re-layouts  2.11 us
  transfers between devices with their start and end apart: 1, of which 1 were waited for; matrix products, arithmetic and copies ran while one was open for 0% of the time, Pallas kernels for 2%

profile of v2, /device:TPU:1, one launch (start us, length us, event | category | flops | bytes accessed | tf_op | source)
XLA Modules:
  0.0 94.3 jit_solution(6858643177358201592)
XLA Ops:
  0.0 3.1 %shard_map.74 = f32[2112,128]{1,0:T(8,128)} custom-call(bf16[128,2048]{1,0:T(8,128)(2,1)} %x_hbm.1, bf16[128,128]{1,0:T(8,128)(2,1)} %b_hbm.1, f32[32,128]{1,0:T(8,128)} %bitcast.12), custom_call_target="tpu_custom_call" | custom-call | tf_op jit(solution)/shard_map/pallas_call | solution.py:186
  3.2 0.0 copy-start.1
  3.2 0.0 copy-start.2
  3.2 0.0 copy-start.3
  3.2 0.0 copy-start.6
  3.2 17.4 %all-to-all-start = ((f32[64,33,1,128]{3,2,1,0:T(1,128)}), f32[64,33,1,128]{3,2,1,0:T(1,128)S(1)}, u32[]{:S(2)}, u32[]{:S(2)}) async-start(f32[64,33,1,128]{3,2,1,0:T(1,128)} %bitcast.2), calls=%async_computation | async-start | bytes 2162688 | tf_op jit(solution)/shard_map/all_to_all | solution.py:194
  20.6 0.0 copy-done.1
  20.6 0.0 copy-done.2
  20.7 0.0 copy-done.3
  20.7 0.0 copy-done.6
  20.7 0.0 copy-start
  20.7 1.0 %copy-done = bf16[128,2048]{1,0:T(8,128)(2,1)S(1)} copy-done((bf16[128,2048]{1,0:T(8,128)(2,1)S(1)}, bf16[128,2048]{1,0:T(8,128)(2,1)}, u32[]{:S(2)}) %copy-start) | copy-done | bytes 524312
  21.7 0.0 copy-start.5
  21.7 1.0 %copy-done.5 = bf16[32,64,128]{2,1,0:T(8,128)(2,1)S(1)} copy-done((bf16[32,64,128]{2,1,0:T(8,128)(2,1)S(1)}, bf16[32,64,128]{2,1,0:T(8,128)(2,1)}, u32[]{:S(2)}) %copy-start.5) | copy-done | bytes 524312
  22.8 1.9 %shard_map.73 = (f32[128,2048]{1,0:T(8,128)S(1)}, f32[128,2048]{1,0:T(8,128)S(1)}, f32[32,128]{1,0:T(8,128)S(1)}) custom-call(bf16[128,2048]{1,0:T(8,128)(2,1)S(1)} %copy-done, bf16[128,128]{1,0:T(8,128)(2,1)S(1)} %copy-done.2, bf16[128,128]{1,0:T(8,128)(2,1)S(1)} %copy-done.1, f32[32,128]{1,0:T(8,128)S(1)} %bitcast.13, f32[1,32]{1,0:T(1,128)S(1)} %bitcast.17, ...), custom_call_target="tpu_custom_call" | custom-call | flops 2147483648 | bytes 16777216 | tf_op jit(solution)/shard_map/pallas_call | solution.py:186
  24.7 22.4 %all-to-all-done = f32[64,33,1,128]{3,2,1,0:T(1,128)S(1)} async-done(((f32[64,33,1,128]{3,2,1,0:T(1,128)}), f32[64,33,1,128]{3,2,1,0:T(1,128)S(1)}, u32[]{:S(2)}, u32[]{:S(2)}) %all-to-all-start) | async-done | bytes 1081376 | tf_op jit(solution)/shard_map/all_to_all | solution.py:194
  47.1 0.1 shard_map.75
  47.2 31.7 %all_to_all.10 = f32[64,32,128]{2,1,0:T(8,128)S(1)} all-to-all(f32[64,32,128]{2,1,0:T(8,128)S(1)} %bitcast.11), channel_id=1, replica_groups={{504,496,488,480,472,464,456,448,440,432,424,416,408,400,392,384,376,36..., dimensions={0} | all-to-all | bytes 2097152 | tf_op jit(solution)/shard_map/all_to_all | solution.py:194
  78.9 0.0 copy-start.4
  78.9 0.5 shard_map.76
  79.4 13.9 %all-gather = f32[8,1,128]{2,1,0:T(1,128)S(1)} all-gather(f32[1,1,128]{2,1,0:T(1,128)S(1)} %bitcast.16), channel_id=1, replica_groups={{7,6,5,4,3,2,1,0},{15,14,13,12,11,10,9,8},{23,22,21,20,19,18,17,16},{31..., dimensions={0}, use_global_device_ids=true | all-gather | bytes 4608 | tf_op jit(solution)/shard_map/all_gather | solution.py:248
  93.3 0.0 copy-done.4
  93.3 1.0 %shard_map.77 = bf16[128,2048]{1,0:T(8,128)(2,1)} custom-call(f32[128,2048]{1,0:T(8,128)S(1)} %get-tuple-element.13.y_ref, f32[8,128]{1,0:T(8,128)S(1)} %bitcast.14, f32[1,2048]{1,0:T(1,128)S(1)} %bitcast.15), custom_call_target="tpu_custom_call" | custom-call | tf_op jit(solution)/shard_map/pallas_call | solution.py:186
Async XLA Ops:
  3.2 17.5 %copy-start.1 = (bf16[128,128]{1,0:T(8,128)(2,1)S(1)}, bf16[128,128]{1,0:T(8,128)(2,1)}, u32[]{:S(2)}) copy-start(bf16[128,128]{1,0:T(8,128)(2,1)} %c_ref.3) | copy-start | bytes 98308
  3.2 17.5 %copy-start.2 = (bf16[128,128]{1,0:T(8,128)(2,1)S(1)}, bf16[128,128]{1,0:T(8,128)(2,1)}, u32[]{:S(2)}) copy-start(bf16[128,128]{1,0:T(8,128)(2,1)} %b_hbm.1) | copy-start | bytes 98308
  3.2 17.5 %copy-start.3 = (f32[128,32]{0,1:T(8,128)S(1)}, f32[128,32]{0,1:T(8,128)}, u32[]{:S(2)}) copy-start(f32[128,32]{0,1:T(8,128)} %param.10) | copy-start | bytes 49156
  3.2 17.5 %copy-start.6 = (f32[32]{0:T(128)S(1)}, f32[32]{0:T(128)}, u32[]{:S(2)}) copy-start(f32[32]{0:T(128)} %param.11) | copy-start | bytes 388
  3.2 43.9 %all-to-all-start = ((f32[64,33,1,128]{3,2,1,0:T(1,128)}), f32[64,33,1,128]{3,2,1,0:T(1,128)S(1)}, u32[]{:S(2)}, u32[]{:S(2)}) async-start(f32[64,33,1,128]{3,2,1,0:T(1,128)} %bitcast.2), calls=%async_computation | async-start | bytes 2162688 | tf_op jit(solution)/shard_map/all_to_all | solution.py:194
  20.7 1.0 %copy-start = (bf16[128,2048]{1,0:T(8,128)(2,1)S(1)}, bf16[128,2048]{1,0:T(8,128)(2,1)}, u32[]{:S(2)}) copy-start(bf16[128,2048]{1,0:T(8,128)(2,1)} %x_hbm.1) | copy-start | bytes 1572868
  21.7 1.0 %copy-start.5 = (bf16[32,64,128]{2,1,0:T(8,128)(2,1)S(1)}, bf16[32,64,128]{2,1,0:T(8,128)(2,1)}, u32[]{:S(2)}) copy-start(bf16[32,64,128]{2,1,0:T(8,128)(2,1)} %init_ref.1) | copy-start | bytes 1572868
  78.9 14.4 %copy-start.4 = (f32[2048]{0:T(1024)S(1)}, f32[2048]{0:T(1024)}, u32[]{:S(2)}) copy-start(f32[2048]{0:T(1024)} %param.13) | copy-start | bytes 24580

commit v3 on v2

--- a/solution.py
+++ b/solution.py
@@ -19,6 +19,7 @@
 WIDTH = PAIRS * 128 // PARTS
 FIRST = [8 * ((SEQ - 1 - k) % 8) + (SEQ - 1 - k) // 8 for k in range(SEQ)]
 SECOND = [SEQ - 1 - k for k in range(SEQ)]
+HEADS = 8
 EPSILON = 1e-05
 INTERPRET = False
 
@@ -160,7 +161,7 @@
         y = inside_ref[:, lanes] + outside * grown_ref[:, lanes]
         y_ref[:, lanes] = y
         total = total + y * y
-    squares_ref[...] = jnp.sum(total.T, axis=0, keepdims=True)
+    squares_ref[...] = jnp.broadcast_to(jnp.sum(total.T, axis=0, keepdims=True), (HEADS, TOK))
 
 
 def norm_kernel(y_ref, squares_ref, gain_ref, out_hbm, out_ref, sems):
@@ -238,14 +239,14 @@
     entries = exchange(entries.reshape(SEQ, ROWS, 128), SECOND)
     y, squares = call(
         output_kernel,
-        (whole, shape((1, TOK), F32)),
+        (whole, shape((HEADS, TOK), F32)),
         c_proj,
         inside,
         grown,
         entries.reshape(SEQ * ROWS, 128),
     )
-    order = list(range(lax.axis_size("head")))[::-1]
-    squares = lax.all_gather(squares, "head", axis=0, tiled=True, axis_index_groups=[order])
+    order = list(range(HEADS))[::-1]
+    squares = lax.all_to_all(squares, "head", 0, 0, tiled=True, axis_index_groups=[order])
     return call(
         norm_kernel,
         shape((TOK, PAIRS * 128), BF16),

time: 94.7 us -> 93.2 us (0.984)
  blocking collectives: 45.6 us -> 44 us
    all_gather x1 -> x0, blocking collectives: 13.9 us -> none  [local(): lax.all_gather(squares, 'head', axis=0, tiled=True, axis_index_groups=[or...]
    all_to_all x0 -> x1, blocking collectives: none -> 12.3 us  [local(): lax.all_to_all(squares, 'head', 0, 0, tiled=True, axis_index_groups=[order])]
where the time goes in v3:
time: 93.2 us; the launch traced here: 92.7 us
  blocking collectives  44 us (47%)
  waiting for transfers between devices  22.4 us (24%)
  starting transfers between devices  17.4 us (19%)
  Pallas kernels  6.69 us (7%)
  local copies, waits for them, and re-layouts  2.11 us (2%)
    all_to_all x1, blocking collectives, exchange(): lax.all_to_all(slices, 'seq', 0, 0, tiled=True, axis_index_groups=[order])  31.7 us
    all_to_all x1, waiting for transfers between devices, exchange(): lax.all_to_all(slices, 'seq', 0, 0, tiled=True, axis_index_groups=[order])  22.4 us
    all_to_all x1, starting transfers between devices, exchange(): lax.all_to_all(slices, 'seq', 0, 0, tiled=True, axis_index_groups=[order])  17.4 us
    all_to_all x1, blocking collectives, local(): lax.all_to_all(squares, 'head', 0, 0, tiled=True, axis_index_groups=[order])  12.3 us
    pallas_call x5, Pallas kernels, call(): pl.pallas_call(kernel, out_shape=outs, interpret=INTERPRET, compiler_para...  6.69 us
    unnamed x14, local copies, waits for them, and re-layouts  2.11 us
  transfers between devices with their start and end apart: 1, of which 1 were waited for; matrix products, arithmetic and copies ran while one was open for 0% of the time, Pallas kernels for 2%

profile of v3, /device:TPU:1, one launch (start us, length us, event | category | flops | bytes accessed | tf_op | source)
XLA Modules:
  0.0 92.7 jit_solution(6726159957626205184)
XLA Ops:
  0.0 3.1 %shard_map.74 = f32[2112,128]{1,0:T(8,128)} custom-call(bf16[128,2048]{1,0:T(8,128)(2,1)} %x_hbm.1, bf16[128,128]{1,0:T(8,128)(2,1)} %b_hbm.1, f32[32,128]{1,0:T(8,128)} %bitcast.14), custom_call_target="tpu_custom_call" | custom-call | tf_op jit(solution)/shard_map/pallas_call | solution.py:187
  3.2 0.0 copy-start.1
  3.2 0.0 copy-start.2
  3.2 0.0 copy-start.3
  3.2 0.0 copy-start.6
  3.2 17.4 %all-to-all-start = ((f32[64,33,1,128]{3,2,1,0:T(1,128)}), f32[64,33,1,128]{3,2,1,0:T(1,128)S(1)}, u32[]{:S(2)}, u32[]{:S(2)}) async-start(f32[64,33,1,128]{3,2,1,0:T(1,128)} %bitcast.2), calls=%async_computation | async-start | bytes 2162688 | tf_op jit(solution)/shard_map/all_to_all | solution.py:195
  20.6 0.0 copy-done.1
  20.6 0.0 copy-done.2
  20.7 0.0 copy-done.3
  20.7 0.0 copy-done.6
  20.7 0.0 copy-start
  20.7 1.0 %copy-done = bf16[128,2048]{1,0:T(8,128)(2,1)S(1)} copy-done((bf16[128,2048]{1,0:T(8,128)(2,1)S(1)}, bf16[128,2048]{1,0:T(8,128)(2,1)}, u32[]{:S(2)}) %copy-start) | copy-done | bytes 524312
  21.7 0.0 copy-start.5
  21.7 1.0 %copy-done.5 = bf16[32,64,128]{2,1,0:T(8,128)(2,1)S(1)} copy-done((bf16[32,64,128]{2,1,0:T(8,128)(2,1)S(1)}, bf16[32,64,128]{2,1,0:T(8,128)(2,1)}, u32[]{:S(2)}) %copy-start.5) | copy-done | bytes 524312
  22.8 1.9 %shard_map.73 = (f32[128,2048]{1,0:T(8,128)S(1)}, f32[128,2048]{1,0:T(8,128)S(1)}, f32[32,128]{1,0:T(8,128)S(1)}) custom-call(bf16[128,2048]{1,0:T(8,128)(2,1)S(1)} %copy-done, bf16[128,128]{1,0:T(8,128)(2,1)S(1)} %copy-done.2, bf16[128,128]{1,0:T(8,128)(2,1)S(1)} %copy-done.1, f32[32,128]{1,0:T(8,128)S(1)} %bitcast.15, f32[1,32]{1,0:T(1,128)S(1)} %bitcast.19, ...), custom_call_target="tpu_custom_call" | custom-call | flops 2147483648 | bytes 16777216 | tf_op jit(solution)/shard_map/pallas_call | solution.py:187
  24.7 22.4 %all-to-all-done = f32[64,33,1,128]{3,2,1,0:T(1,128)S(1)} async-done(((f32[64,33,1,128]{3,2,1,0:T(1,128)}), f32[64,33,1,128]{3,2,1,0:T(1,128)S(1)}, u32[]{:S(2)}, u32[]{:S(2)}) %all-to-all-start) | async-done | bytes 1081376 | tf_op jit(solution)/shard_map/all_to_all | solution.py:195
  47.1 0.1 shard_map.75
  47.2 31.7 %all_to_all.21 = f32[64,32,128]{2,1,0:T(8,128)S(1)} all-to-all(f32[64,32,128]{2,1,0:T(8,128)S(1)} %bitcast.13), channel_id=1, replica_groups={{504,496,488,480,472,464,456,448,440,432,424,416,408,400,392,384,376,36..., dimensions={0} | all-to-all | bytes 2097152 | tf_op jit(solution)/shard_map/all_to_all | solution.py:195
  78.9 0.0 copy-start.4
  78.9 0.5 shard_map.76
  79.4 12.3 %all_to_all.22 = f32[8,1,128]{2,1,0:T(1,128)S(1)} all-to-all(f32[8,1,128]{2,1,0:T(1,128)S(1)} %bitcast.18), channel_id=1, replica_groups={{7,6,5,4,3,2,1,0},{15,14,13,12,11,10,9,8},{23,22,21,20,19,18,17,16},{31..., dimensions={0} | all-to-all | bytes 8192 | tf_op jit(solution)/shard_map/all_to_all | solution.py:249
  91.7 0.0 copy-done.4
  91.7 1.0 %shard_map.77 = bf16[128,2048]{1,0:T(8,128)(2,1)} custom-call(f32[128,2048]{1,0:T(8,128)S(1)} %get-tuple-element.13.y_ref, f32[8,128]{1,0:T(8,128)S(1)} %bitcast.16, f32[1,2048]{1,0:T(1,128)S(1)} %bitcast.17), custom_call_target="tpu_custom_call" | custom-call | tf_op jit(solution)/shard_map/pallas_call | solution.py:187
Async XLA Ops:
  3.2 17.5 %copy-start.1 = (bf16[128,128]{1,0:T(8,128)(2,1)S(1)}, bf16[128,128]{1,0:T(8,128)(2,1)}, u32[]{:S(2)}) copy-start(bf16[128,128]{1,0:T(8,128)(2,1)} %c_ref.3) | copy-start | bytes 98308
  3.2 17.5 %copy-start.2 = (bf16[128,128]{1,0:T(8,128)(2,1)S(1)}, bf16[128,128]{1,0:T(8,128)(2,1)}, u32[]{:S(2)}) copy-start(bf16[128,128]{1,0:T(8,128)(2,1)} %b_hbm.1) | copy-start | bytes 98308
  3.2 17.5 %copy-start.3 = (f32[128,32]{0,1:T(8,128)S(1)}, f32[128,32]{0,1:T(8,128)}, u32[]{:S(2)}) copy-start(f32[128,32]{0,1:T(8,128)} %param.10) | copy-start | bytes 49156
  3.2 17.5 %copy-start.6 = (f32[32]{0:T(128)S(1)}, f32[32]{0:T(128)}, u32[]{:S(2)}) copy-start(f32[32]{0:T(128)} %param.11) | copy-start | bytes 388
  3.2 43.9 %all-to-all-start = ((f32[64,33,1,128]{3,2,1,0:T(1,128)}), f32[64,33,1,128]{3,2,1,0:T(1,128)S(1)}, u32[]{:S(2)}, u32[]{:S(2)}) async-start(f32[64,33,1,128]{3,2,1,0:T(1,128)} %bitcast.2), calls=%async_computation | async-start | bytes 2162688 | tf_op jit(solution)/shard_map/all_to_all | solution.py:195
  20.7 1.0 %copy-start = (bf16[128,2048]{1,0:T(8,128)(2,1)S(1)}, bf16[128,2048]{1,0:T(8,128)(2,1)}, u32[]{:S(2)}) copy-start(bf16[128,2048]{1,0:T(8,128)(2,1)} %x_hbm.1) | copy-start | bytes 1572868
  21.7 1.0 %copy-start.5 = (bf16[32,64,128]{2,1,0:T(8,128)(2,1)S(1)}, bf16[32,64,128]{2,1,0:T(8,128)(2,1)}, u32[]{:S(2)}) copy-start(bf16[32,64,128]{2,1,0:T(8,128)(2,1)} %init_ref.1) | copy-start | bytes 1572868
  78.9 12.8 %copy-start.4 = (f32[2048]{0:T(1024)S(1)}, f32[2048]{0:T(1024)}, u32[]{:S(2)}) copy-start(f32[2048]{0:T(1024)} %param.13) | copy-start | bytes 24580

commit v4 on v3

--- a/solution.py
+++ b/solution.py
@@ -245,7 +245,7 @@
         grown,
         entries.reshape(SEQ * ROWS, 128),
     )
-    order = list(range(HEADS))[::-1]
+    order = [(HEADS - 3 - k) % HEADS for k in range(HEADS)]
     squares = lax.all_to_all(squares, "head", 0, 0, tiled=True, axis_index_groups=[order])
     return call(
         norm_kernel,

time: 93.2 us -> 92.3 us (level)
  no operation moved by 1% of the time
where the time goes in v4:
time: 92.3 us; the launch traced here: 91.9 us
  blocking collectives  43.1 us (47%)
  waiting for transfers between devices  22.4 us (24%)
  starting transfers between devices  17.4 us (19%)
  Pallas kernels  6.69 us (7%)
  local copies, waits for them, and re-layouts  2.11 us (2%)
    all_to_all x1, blocking collectives, exchange(): lax.all_to_all(slices, 'seq', 0, 0, tiled=True, axis_index_groups=[order])  31.7 us
    all_to_all x1, waiting for transfers between devices, exchange(): lax.all_to_all(slices, 'seq', 0, 0, tiled=True, axis_index_groups=[order])  22.4 us
    all_to_all x1, starting transfers between devices, exchange(): lax.all_to_all(slices, 'seq', 0, 0, tiled=True, axis_index_groups=[order])  17.4 us
    all_to_all x1, blocking collectives, local(): lax.all_to_all(squares, 'head', 0, 0, tiled=True, axis_index_groups=[order])  11.5 us
    pallas_call x5, Pallas kernels, call(): pl.pallas_call(kernel, out_shape=outs, interpret=INTERPRET, compiler_para...  6.69 us
    unnamed x14, local copies, waits for them, and re-layouts  2.11 us
  transfers between devices with their start and end apart: 1, of which 1 were waited for; matrix products, arithmetic and copies ran while one was open for 0% of the time, Pallas kernels for 2%

profile of v4, /device:TPU:1, one launch (start us, length us, event | category | flops | bytes accessed | tf_op | source)
XLA Modules:
  0.0 91.9 jit_solution(3480928442030684263)
XLA Ops:
  0.0 3.1 %shard_map.74 = f32[2112,128]{1,0:T(8,128)} custom-call(bf16[128,2048]{1,0:T(8,128)(2,1)} %x_hbm.1, bf16[128,128]{1,0:T(8,128)(2,1)} %b_hbm.1, f32[32,128]{1,0:T(8,128)} %bitcast.14), custom_call_target="tpu_custom_call" | custom-call | tf_op jit(solution)/shard_map/pallas_call | solution.py:187
  3.2 0.0 copy-start.1
  3.2 0.0 copy-start.2
  3.2 0.0 copy-start.3
  3.2 0.0 copy-start.6
  3.2 17.4 %all-to-all-start = ((f32[64,33,1,128]{3,2,1,0:T(1,128)}), f32[64,33,1,128]{3,2,1,0:T(1,128)S(1)}, u32[]{:S(2)}, u32[]{:S(2)}) async-start(f32[64,33,1,128]{3,2,1,0:T(1,128)} %bitcast.2), calls=%async_computation | async-start | bytes 2162688 | tf_op jit(solution)/shard_map/all_to_all | solution.py:195
  20.6 0.0 copy-done.1
  20.6 0.0 copy-done.2
  20.7 0.0 copy-done.3
  20.7 0.0 copy-done.6
  20.7 0.0 copy-start
  20.7 1.0 %copy-done = bf16[128,2048]{1,0:T(8,128)(2,1)S(1)} copy-done((bf16[128,2048]{1,0:T(8,128)(2,1)S(1)}, bf16[128,2048]{1,0:T(8,128)(2,1)}, u32[]{:S(2)}) %copy-start) | copy-done | bytes 524312
  21.7 0.0 copy-start.5
  21.7 1.0 %copy-done.5 = bf16[32,64,128]{2,1,0:T(8,128)(2,1)S(1)} copy-done((bf16[32,64,128]{2,1,0:T(8,128)(2,1)S(1)}, bf16[32,64,128]{2,1,0:T(8,128)(2,1)}, u32[]{:S(2)}) %copy-start.5) | copy-done | bytes 524312
  22.8 1.9 %shard_map.73 = (f32[128,2048]{1,0:T(8,128)S(1)}, f32[128,2048]{1,0:T(8,128)S(1)}, f32[32,128]{1,0:T(8,128)S(1)}) custom-call(bf16[128,2048]{1,0:T(8,128)(2,1)S(1)} %copy-done, bf16[128,128]{1,0:T(8,128)(2,1)S(1)} %copy-done.2, bf16[128,128]{1,0:T(8,128)(2,1)S(1)} %copy-done.1, f32[32,128]{1,0:T(8,128)S(1)} %bitcast.15, f32[1,32]{1,0:T(1,128)S(1)} %bitcast.19, ...), custom_call_target="tpu_custom_call" | custom-call | flops 2147483648 | bytes 16777216 | tf_op jit(solution)/shard_map/pallas_call | solution.py:187
  24.7 22.4 %all-to-all-done = f32[64,33,1,128]{3,2,1,0:T(1,128)S(1)} async-done(((f32[64,33,1,128]{3,2,1,0:T(1,128)}), f32[64,33,1,128]{3,2,1,0:T(1,128)S(1)}, u32[]{:S(2)}, u32[]{:S(2)}) %all-to-all-start) | async-done | bytes 1081376 | tf_op jit(solution)/shard_map/all_to_all | solution.py:195
  47.1 0.1 shard_map.75
  47.2 31.7 %all_to_all.21 = f32[64,32,128]{2,1,0:T(8,128)S(1)} all-to-all(f32[64,32,128]{2,1,0:T(8,128)S(1)} %bitcast.13), channel_id=1, replica_groups={{504,496,488,480,472,464,456,448,440,432,424,416,408,400,392,384,376,36..., dimensions={0} | all-to-all | bytes 2097152 | tf_op jit(solution)/shard_map/all_to_all | solution.py:195
  78.9 0.0 copy-start.4
  78.9 0.5 shard_map.76
  79.4 11.5 %all_to_all.22 = f32[8,1,128]{2,1,0:T(1,128)S(1)} all-to-all(f32[8,1,128]{2,1,0:T(1,128)S(1)} %bitcast.18), channel_id=1, replica_groups={{5,4,3,2,1,0,7,6},{13,12,11,10,9,8,15,14},{21,20,19,18,17,16,23,22},{29..., dimensions={0} | all-to-all | bytes 8192 | tf_op jit(solution)/shard_map/all_to_all | solution.py:249
  90.9 0.0 copy-done.4
  90.9 1.0 %shard_map.77 = bf16[128,2048]{1,0:T(8,128)(2,1)} custom-call(f32[128,2048]{1,0:T(8,128)S(1)} %get-tuple-element.13.y_ref, f32[8,128]{1,0:T(8,128)S(1)} %bitcast.16, f32[1,2048]{1,0:T(1,128)S(1)} %bitcast.17), custom_call_target="tpu_custom_call" | custom-call | tf_op jit(solution)/shard_map/pallas_call | solution.py:187
Async XLA Ops:
  3.2 17.5 %copy-start.1 = (bf16[128,128]{1,0:T(8,128)(2,1)S(1)}, bf16[128,128]{1,0:T(8,128)(2,1)}, u32[]{:S(2)}) copy-start(bf16[128,128]{1,0:T(8,128)(2,1)} %c_ref.3) | copy-start | bytes 98308
  3.2 17.5 %copy-start.2 = (bf16[128,128]{1,0:T(8,128)(2,1)S(1)}, bf16[128,128]{1,0:T(8,128)(2,1)}, u32[]{:S(2)}) copy-start(bf16[128,128]{1,0:T(8,128)(2,1)} %b_hbm.1) | copy-start | bytes 98308
  3.2 17.5 %copy-start.3 = (f32[128,32]{0,1:T(8,128)S(1)}, f32[128,32]{0,1:T(8,128)}, u32[]{:S(2)}) copy-start(f32[128,32]{0,1:T(8,128)} %param.10) | copy-start | bytes 49156
  3.2 17.5 %copy-start.6 = (f32[32]{0:T(128)S(1)}, f32[32]{0:T(128)}, u32[]{:S(2)}) copy-start(f32[32]{0:T(128)} %param.11) | copy-start | bytes 388
  3.2 43.9 %all-to-all-start = ((f32[64,33,1,128]{3,2,1,0:T(1,128)}), f32[64,33,1,128]{3,2,1,0:T(1,128)S(1)}, u32[]{:S(2)}, u32[]{:S(2)}) async-start(f32[64,33,1,128]{3,2,1,0:T(1,128)} %bitcast.2), calls=%async_computation | async-start | bytes 2162688 | tf_op jit(solution)/shard_map/all_to_all | solution.py:195
  20.7 1.0 %copy-start = (bf16[128,2048]{1,0:T(8,128)(2,1)S(1)}, bf16[128,2048]{1,0:T(8,128)(2,1)}, u32[]{:S(2)}) copy-start(bf16[128,2048]{1,0:T(8,128)(2,1)} %x_hbm.1) | copy-start | bytes 1572868
  21.7 1.0 %copy-start.5 = (bf16[32,64,128]{2,1,0:T(8,128)(2,1)S(1)}, bf16[32,64,128]{2,1,0:T(8,128)(2,1)}, u32[]{:S(2)}) copy-start(bf16[32,64,128]{2,1,0:T(8,128)(2,1)} %init_ref.1) | copy-start | bytes 1572868
  78.9 12.0 %copy-start.4 = (f32[2048]{0:T(1024)S(1)}, f32[2048]{0:T(1024)}, u32[]{:S(2)}) copy-start(f32[2048]{0:T(1024)} %param.13) | copy-start | bytes 24580

commit v5 on v4

--- a/solution.py
+++ b/solution.py
@@ -52,26 +52,24 @@
         pltpu.make_async_copy(decay_hbm, decay_ref, sems.at[0]),
         pltpu.make_async_copy(b_hbm, b_ref, sems.at[1]),
     ]
-    for part in range(PARTS):
-        lanes = pl.ds(WIDTH * part, WIDTH)
-        copies.append(
-            pltpu.make_async_copy(x_hbm.at[:, lanes], x_ref.at[:, lanes], sems.at[2 + part])
-        )
+    copies.append(pltpu.make_async_copy(x_hbm, x_ref, sems.at[2]))
     for copy in copies:
         copy.start()
     row, col = iotas((TOK, TOK))
     copies[0].wait()
-    after = summed(decay_ref, row > col).T
+    after = summed(decay_ref, row > col)
     to_end = jnp.exp(after)
-    total = after[0:1] + decay_ref[...].T[0:1]
+    total = (after + decay_ref[...]).T[0:1]
     copies[1].wait()
-    keys = b_ref[...].astype(F32).T.astype(BF16)
-    for pair in range(PAIRS):
-        if pair % (PAIRS // PARTS) == 0:
-            copies[2 + pair // (PAIRS // PARTS)].wait()
-        lanes = slice(128 * pair, 128 * pair + 128)
-        carried = (x_ref[:, lanes].astype(F32) * by_head(to_end, pair)).astype(BF16)
-        state = jnp.dot(keys, carried, preferred_element_type=F32)
+    keys = b_ref[...].astype(F32).T
+    copies[2].wait()
+    for pair in range(PAIRS):
+        x = x_ref[:, 128 * pair : 128 * pair + 128]
+        state = [
+            jnp.dot((keys * to_end[h : h + 1]).astype(BF16), half, preferred_element_type=F32)
+            for h, half in ((2 * pair, x[:, :HEAD_DIM]), (2 * pair + 1, x[:, HEAD_DIM:]))
+        ]
+        state = jnp.concatenate(state, axis=1)
         total_row = by_head(total, pair)
         for cut in range(CUT):
             base = SENT * (CUT * pair + cut)
@@ -84,7 +82,7 @@
                 pltpu.make_async_copy(out_ref.at[rows], out_hbm.at[rows], out_sems.at[part])
             )
             copies[-1].start()
-    for copy in copies[2 + PARTS :]:
+    for copy in copies[3:]:
         copy.wait()
 
 
@@ -213,7 +211,7 @@
             pltpu.VMEM(b_proj.shape, BF16),
             pltpu.VMEM(decay.shape, F32),
             pltpu.VMEM((SEQ * SENT, 128), F32),
-            pltpu.SemaphoreType.DMA((2 + PARTS,)),
+            pltpu.SemaphoreType.DMA((3,)),
             pltpu.SemaphoreType.DMA((PARTS,)),
         ],
     )

time: 92.3 us -> 91.9 us (level)
  no operation moved by 1% of the time
where the time goes in v5:
time: 91.9 us; the launch traced here: 91.4 us
  blocking collectives  43.1 us (47%)
  waiting for transfers between devices  22.4 us (24%)
  starting transfers between devices  17.4 us (19%)
  Pallas kernels  6.21 us (7%)
  local copies, waits for them, and re-layouts  2.11 us (2%)
    all_to_all x1, blocking collectives, exchange(): lax.all_to_all(slices, 'seq', 0, 0, tiled=True, axis_index_groups=[order])  31.7 us
    all_to_all x1, waiting for transfers between devices, exchange(): lax.all_to_all(slices, 'seq', 0, 0, tiled=True, axis_index_groups=[order])  22.4 us
    all_to_all x1, starting transfers between devices, exchange(): lax.all_to_all(slices, 'seq', 0, 0, tiled=True, axis_index_groups=[order])  17.4 us
    all_to_all x1, blocking collectives, local(): lax.all_to_all(squares, 'head', 0, 0, tiled=True, axis_index_groups=[order])  11.5 us
    pallas_call x5, Pallas kernels, call(): pl.pallas_call(kernel, out_shape=outs, interpret=INTERPRET, compiler_para...  6.21 us
    unnamed x14, local copies, waits for them, and re-layouts  2.11 us
  transfers between devices with their start and end apart: 1, of which 1 were waited for; matrix products, arithmetic and copies ran while one was open for 0% of the time, Pallas kernels for 2%

profile of v5, /device:TPU:1, one launch (start us, length us, event | category | flops | bytes accessed | tf_op | source)
XLA Modules:
  0.0 91.4 jit_solution(956570160472557812)
XLA Ops:
  0.0 2.7 %shard_map.74 = f32[2112,128]{1,0:T(8,128)} custom-call(bf16[128,2048]{1,0:T(8,128)(2,1)} %x_hbm.1, bf16[128,128]{1,0:T(8,128)(2,1)} %b_hbm.1, f32[32,128]{1,0:T(8,128)} %bitcast.14), custom_call_target="tpu_custom_call" | custom-call | tf_op jit(solution)/shard_map/pallas_call | solution.py:185
  2.7 0.0 copy-start.1
  2.7 0.0 copy-start.2
  2.7 0.0 copy-start.3
  2.7 0.0 copy-start.6
  2.7 17.4 %all-to-all-start = ((f32[64,33,1,128]{3,2,1,0:T(1,128)}), f32[64,33,1,128]{3,2,1,0:T(1,128)S(1)}, u32[]{:S(2)}, u32[]{:S(2)}) async-start(f32[64,33,1,128]{3,2,1,0:T(1,128)} %bitcast.2), calls=%async_computation | async-start | bytes 2162688 | tf_op jit(solution)/shard_map/all_to_all | solution.py:193
  20.1 0.0 copy-done.1
  20.2 0.0 copy-done.2
  20.2 0.0 copy-done.3
  20.2 0.0 copy-done.6
  20.2 0.0 copy-start
  20.2 1.0 %copy-done = bf16[128,2048]{1,0:T(8,128)(2,1)S(1)} copy-done((bf16[128,2048]{1,0:T(8,128)(2,1)S(1)}, bf16[128,2048]{1,0:T(8,128)(2,1)}, u32[]{:S(2)}) %copy-start) | copy-done | bytes 524312
  21.2 0.0 copy-start.5
  21.2 1.0 %copy-done.5 = bf16[32,64,128]{2,1,0:T(8,128)(2,1)S(1)} copy-done((bf16[32,64,128]{2,1,0:T(8,128)(2,1)S(1)}, bf16[32,64,128]{2,1,0:T(8,128)(2,1)}, u32[]{:S(2)}) %copy-start.5) | copy-done | bytes 524312
  22.3 1.9 %shard_map.73 = (f32[128,2048]{1,0:T(8,128)S(1)}, f32[128,2048]{1,0:T(8,128)S(1)}, f32[32,128]{1,0:T(8,128)S(1)}) custom-call(bf16[128,2048]{1,0:T(8,128)(2,1)S(1)} %copy-done, bf16[128,128]{1,0:T(8,128)(2,1)S(1)} %copy-done.2, bf16[128,128]{1,0:T(8,128)(2,1)S(1)} %copy-done.1, f32[32,128]{1,0:T(8,128)S(1)} %bitcast.15, f32[1,32]{1,0:T(1,128)S(1)} %bitcast.19, ...), custom_call_target="tpu_custom_call" | custom-call | flops 2147483648 | bytes 16777216 | tf_op jit(solution)/shard_map/pallas_call | solution.py:185
  24.2 22.4 %all-to-all-done = f32[64,33,1,128]{3,2,1,0:T(1,128)S(1)} async-done(((f32[64,33,1,128]{3,2,1,0:T(1,128)}), f32[64,33,1,128]{3,2,1,0:T(1,128)S(1)}, u32[]{:S(2)}, u32[]{:S(2)}) %all-to-all-start) | async-done | bytes 1081376 | tf_op jit(solution)/shard_map/all_to_all | solution.py:193
  46.6 0.1 shard_map.75
  46.7 31.7 %all_to_all.21 = f32[64,32,128]{2,1,0:T(8,128)S(1)} all-to-all(f32[64,32,128]{2,1,0:T(8,128)S(1)} %bitcast.13), channel_id=1, replica_groups={{504,496,488,480,472,464,456,448,440,432,424,416,408,400,392,384,376,36..., dimensions={0} | all-to-all | bytes 2097152 | tf_op jit(solution)/shard_map/all_to_all | solution.py:193
  78.4 0.0 copy-start.4
  78.4 0.5 shard_map.76
  78.9 11.5 %all_to_all.22 = f32[8,1,128]{2,1,0:T(1,128)S(1)} all-to-all(f32[8,1,128]{2,1,0:T(1,128)S(1)} %bitcast.18), channel_id=1, replica_groups={{5,4,3,2,1,0,7,6},{13,12,11,10,9,8,15,14},{21,20,19,18,17,16,23,22},{29..., dimensions={0} | all-to-all | bytes 8192 | tf_op jit(solution)/shard_map/all_to_all | solution.py:247
  90.4 0.0 copy-done.4
  90.4 1.0 %shard_map.77 = bf16[128,2048]{1,0:T(8,128)(2,1)} custom-call(f32[128,2048]{1,0:T(8,128)S(1)} %get-tuple-element.13.y_ref, f32[8,128]{1,0:T(8,128)S(1)} %bitcast.16, f32[1,2048]{1,0:T(1,128)S(1)} %bitcast.17), custom_call_target="tpu_custom_call" | custom-call | tf_op jit(solution)/shard_map/pallas_call | solution.py:185
Async XLA Ops:
  2.7 17.5 %copy-start.1 = (bf16[128,128]{1,0:T(8,128)(2,1)S(1)}, bf16[128,128]{1,0:T(8,128)(2,1)}, u32[]{:S(2)}) copy-start(bf16[128,128]{1,0:T(8,128)(2,1)} %c_ref.3) | copy-start | bytes 98308
  2.7 17.5 %copy-start.2 = (bf16[128,128]{1,0:T(8,128)(2,1)S(1)}, bf16[128,128]{1,0:T(8,128)(2,1)}, u32[]{:S(2)}) copy-start(bf16[128,128]{1,0:T(8,128)(2,1)} %b_hbm.1) | copy-start | bytes 98308
  2.7 17.5 %copy-start.3 = (f32[128,32]{0,1:T(8,128)S(1)}, f32[128,32]{0,1:T(8,128)}, u32[]{:S(2)}) copy-start(f32[128,32]{0,1:T(8,128)} %param.10) | copy-start | bytes 49156
  2.7 17.5 %copy-start.6 = (f32[32]{0:T(128)S(1)}, f32[32]{0:T(128)}, u32[]{:S(2)}) copy-start(f32[32]{0:T(128)} %param.11) | copy-start | bytes 388
  2.7 43.9 %all-to-all-start = ((f32[64,33,1,128]{3,2,1,0:T(1,128)}), f32[64,33,1,128]{3,2,1,0:T(1,128)S(1)}, u32[]{:S(2)}, u32[]{:S(2)}) async-start(f32[64,33,1,128]{3,2,1,0:T(1,128)} %bitcast.2), calls=%async_computation | async-start | bytes 2162688 | tf_op jit(solution)/shard_map/all_to_all | solution.py:193
  20.2 1.0 %copy-start = (bf16[128,2048]{1,0:T(8,128)(2,1)S(1)}, bf16[128,2048]{1,0:T(8,128)(2,1)}, u32[]{:S(2)}) copy-start(bf16[128,2048]{1,0:T(8,128)(2,1)} %x_hbm.1) | copy-start | bytes 1572868
  21.2 1.0 %copy-start.5 = (bf16[32,64,128]{2,1,0:T(8,128)(2,1)S(1)}, bf16[32,64,128]{2,1,0:T(8,128)(2,1)}, u32[]{:S(2)}) copy-start(bf16[32,64,128]{2,1,0:T(8,128)(2,1)} %init_ref.1) | copy-start | bytes 1572868
  78.4 12.0 %copy-start.4 = (f32[2048]{0:T(1024)S(1)}, f32[2048]{0:T(1024)}, u32[]{:S(2)}) copy-start(f32[2048]{0:T(1024)} %param.13) | copy-start | bytes 24580

commit v6 on v4

--- a/solution.py
+++ b/solution.py
@@ -52,11 +52,7 @@
         pltpu.make_async_copy(decay_hbm, decay_ref, sems.at[0]),
         pltpu.make_async_copy(b_hbm, b_ref, sems.at[1]),
     ]
-    for part in range(PARTS):
-        lanes = pl.ds(WIDTH * part, WIDTH)
-        copies.append(
-            pltpu.make_async_copy(x_hbm.at[:, lanes], x_ref.at[:, lanes], sems.at[2 + part])
-        )
+    copies.append(pltpu.make_async_copy(x_hbm, x_ref, sems.at[2]))
     for copy in copies:
         copy.start()
     row, col = iotas((TOK, TOK))
@@ -66,9 +62,8 @@
     total = after[0:1] + decay_ref[...].T[0:1]
     copies[1].wait()
     keys = b_ref[...].astype(F32).T.astype(BF16)
-    for pair in range(PAIRS):
-        if pair % (PAIRS // PARTS) == 0:
-            copies[2 + pair // (PAIRS // PARTS)].wait()
+    copies[2].wait()
+    for pair in range(PAIRS):
         lanes = slice(128 * pair, 128 * pair + 128)
         carried = (x_ref[:, lanes].astype(F32) * by_head(to_end, pair)).astype(BF16)
         state = jnp.dot(keys, carried, preferred_element_type=F32)
@@ -84,7 +79,7 @@
                 pltpu.make_async_copy(out_ref.at[rows], out_hbm.at[rows], out_sems.at[part])
             )
             copies[-1].start()
-    for copy in copies[2 + PARTS :]:
+    for copy in copies[3:]:
         copy.wait()
 
 
@@ -147,7 +142,7 @@
         inside_ref[:, lanes] = inside + by_head(skip, pair) * x.astype(F32)
 
 
-def output_kernel(c_ref, inside_ref, grown_ref, entry_ref, y_ref, squares_ref):
+def output_kernel(c_ref, inside_ref, grown_ref, gain_ref, entry_ref, y_ref, squares_ref):
     query = c_ref[...]
     twice = jnp.concatenate([query, query], axis=1)
     total = jnp.zeros((TOK, 128), F32)
@@ -159,18 +154,18 @@
         rest = (entry - high.astype(F32)).astype(BF16)
         outside = jnp.dot(twice, jnp.concatenate([high, rest], axis=0), preferred_element_type=F32)
         y = inside_ref[:, lanes] + outside * grown_ref[:, lanes]
-        y_ref[:, lanes] = y
+        y_ref[:, lanes] = y * gain_ref[:, lanes]
         total = total + y * y
     squares_ref[...] = jnp.broadcast_to(jnp.sum(total.T, axis=0, keepdims=True), (HEADS, TOK))
 
 
-def norm_kernel(y_ref, squares_ref, gain_ref, out_hbm, out_ref, sems):
+def norm_kernel(y_ref, squares_ref, out_hbm, out_ref, sems):
     mean = jnp.sum(squares_ref[...], axis=0, keepdims=True) / (RECURRENT_UNITS * HEAD_DIM)
     copies = []
     factor = jnp.broadcast_to(lax.rsqrt(mean + EPSILON), (TOK, TOK)).T
     for pair in range(PAIRS):
         lanes = slice(128 * pair, 128 * pair + 128)
-        out_ref[:, lanes] = (y_ref[:, lanes] * factor * gain_ref[:, lanes]).astype(BF16)
+        out_ref[:, lanes] = (y_ref[:, lanes] * factor).astype(BF16)
         if (pair + 1) % (PAIRS // PARTS) == 0:
             part = pair // (PAIRS // PARTS)
             lanes = pl.ds(WIDTH * part, WIDTH)
@@ -213,7 +208,7 @@
             pltpu.VMEM(b_proj.shape, BF16),
             pltpu.VMEM(decay.shape, F32),
             pltpu.VMEM((SEQ * SENT, 128), F32),
-            pltpu.SemaphoreType.DMA((2 + PARTS,)),
+            pltpu.SemaphoreType.DMA((3,)),
             pltpu.SemaphoreType.DMA((PARTS,)),
         ],
     )
@@ -243,6 +238,7 @@
         c_proj,
         inside,
         grown,
+        norm_gain.reshape(1, -1),
         entries.reshape(SEQ * ROWS, 128),
     )
     order = [(HEADS - 3 - k) % HEADS for k in range(HEADS)]
@@ -252,7 +248,6 @@
         shape((TOK, PAIRS * 128), BF16),
         y,
         squares,
-        norm_gain.reshape(1, -1),
         out_specs=anywhere,
         scratch_shapes=[pltpu.VMEM((TOK, PAIRS * 128), BF16), pltpu.SemaphoreType.DMA((PARTS,))],
     )

time: 92.3 us -> 92.1 us (level)
  no operation moved by 1% of the time
where the time goes in v6:
time: 92.1 us; the launch traced here: 91.6 us
  blocking collectives  43.1 us (47%)
  waiting for transfers between devices  22.4 us (24%)
  starting transfers between devices  17.4 us (19%)
  Pallas kernels  6.43 us (7%)
  local copies, waits for them, and re-layouts  2.11 us (2%)
    all_to_all x1, blocking collectives, exchange(): lax.all_to_all(slices, 'seq', 0, 0, tiled=True, axis_index_groups=[order])  31.7 us
    all_to_all x1, waiting for transfers between devices, exchange(): lax.all_to_all(slices, 'seq', 0, 0, tiled=True, axis_index_groups=[order])  22.4 us
    all_to_all x1, starting transfers between devices, exchange(): lax.all_to_all(slices, 'seq', 0, 0, tiled=True, axis_index_groups=[order])  17.4 us
    all_to_all x1, blocking collectives, local(): lax.all_to_all(squares, 'head', 0, 0, tiled=True, axis_index_groups=[order])  11.5 us
    pallas_call x5, Pallas kernels, call(): pl.pallas_call(kernel, out_shape=outs, interpret=INTERPRET, compiler_para...  6.43 us
    unnamed x14, local copies, waits for them, and re-layouts  2.11 us
  transfers between devices with their start and end apart: 1, of which 1 were waited for; matrix products, arithmetic and copies ran while one was open for 0% of the time, Pallas kernels for 2%

profile of v6, /device:TPU:1, one launch (start us, length us, event | category | flops | bytes accessed | tf_op | source)
XLA Modules:
  0.0 91.6 jit_solution(13351832193450393626)
XLA Ops:
  0.0 2.9 %shard_map.74 = f32[2112,128]{1,0:T(8,128)} custom-call(bf16[128,2048]{1,0:T(8,128)(2,1)} %x_hbm.1, bf16[128,128]{1,0:T(8,128)(2,1)} %b_hbm.1, f32[32,128]{1,0:T(8,128)} %bitcast.14), custom_call_target="tpu_custom_call" | custom-call | tf_op jit(solution)/shard_map/pallas_call | solution.py:182
  2.9 0.0 copy-start.1
  2.9 0.0 copy-start.2
  2.9 0.0 copy-start.3
  3.0 0.0 copy-start.6
  3.0 17.4 %all-to-all-start = ((f32[64,33,1,128]{3,2,1,0:T(1,128)}), f32[64,33,1,128]{3,2,1,0:T(1,128)S(1)}, u32[]{:S(2)}, u32[]{:S(2)}) async-start(f32[64,33,1,128]{3,2,1,0:T(1,128)} %bitcast.3), calls=%async_computation | async-start | bytes 2162688 | tf_op jit(solution)/shard_map/all_to_all | solution.py:190
  20.4 0.0 copy-done.1
  20.4 0.0 copy-done.2
  20.4 0.0 copy-done.3
  20.4 0.0 copy-done.6
  20.4 0.0 copy-start
  20.4 1.0 %copy-done = bf16[128,2048]{1,0:T(8,128)(2,1)S(1)} copy-done((bf16[128,2048]{1,0:T(8,128)(2,1)S(1)}, bf16[128,2048]{1,0:T(8,128)(2,1)}, u32[]{:S(2)}) %copy-start) | copy-done | bytes 524312
  21.5 0.0 copy-start.5
  21.5 1.0 %copy-done.5 = bf16[32,64,128]{2,1,0:T(8,128)(2,1)S(1)} copy-done((bf16[32,64,128]{2,1,0:T(8,128)(2,1)S(1)}, bf16[32,64,128]{2,1,0:T(8,128)(2,1)}, u32[]{:S(2)}) %copy-start.5) | copy-done | bytes 524312
  22.5 1.9 %shard_map.73 = (f32[128,2048]{1,0:T(8,128)S(1)}, f32[128,2048]{1,0:T(8,128)S(1)}, f32[32,128]{1,0:T(8,128)S(1)}) custom-call(bf16[128,2048]{1,0:T(8,128)(2,1)S(1)} %copy-done, bf16[128,128]{1,0:T(8,128)(2,1)S(1)} %copy-done.2, bf16[128,128]{1,0:T(8,128)(2,1)S(1)} %copy-done.1, f32[32,128]{1,0:T(8,128)S(1)} %bitcast.15, f32[1,32]{1,0:T(1,128)S(1)} %bitcast.19, ...), custom_call_target="tpu_custom_call" | custom-call | flops 2147483648 | bytes 16777216 | tf_op jit(solution)/shard_map/pallas_call | solution.py:182
  24.4 22.4 %all-to-all-done = f32[64,33,1,128]{3,2,1,0:T(1,128)S(1)} async-done(((f32[64,33,1,128]{3,2,1,0:T(1,128)}), f32[64,33,1,128]{3,2,1,0:T(1,128)S(1)}, u32[]{:S(2)}, u32[]{:S(2)}) %all-to-all-start) | async-done | bytes 1081376 | tf_op jit(solution)/shard_map/all_to_all | solution.py:190
  46.8 0.1 shard_map.75
  47.0 0.0 copy-start.4
  47.0 31.7 %all_to_all.21 = f32[64,32,128]{2,1,0:T(8,128)S(1)} all-to-all(f32[64,32,128]{2,1,0:T(8,128)S(1)} %bitcast.13), channel_id=1, replica_groups={{504,496,488,480,472,464,456,448,440,432,424,416,408,400,392,384,376,36..., dimensions={0} | all-to-all | bytes 2097152 | tf_op jit(solution)/shard_map/all_to_all | solution.py:190
  78.7 0.0 copy-done.4
  78.7 0.5 shard_map.76
  79.2 11.5 %all_to_all.22 = f32[8,1,128]{2,1,0:T(1,128)S(1)} all-to-all(f32[8,1,128]{2,1,0:T(1,128)S(1)} %bitcast.18), channel_id=1, replica_groups={{5,4,3,2,1,0,7,6},{13,12,11,10,9,8,15,14},{21,20,19,18,17,16,23,22},{29..., dimensions={0} | all-to-all | bytes 8192 | tf_op jit(solution)/shard_map/all_to_all | solution.py:245
  90.7 1.0 %shard_map.77 = bf16[128,2048]{1,0:T(8,128)(2,1)} custom-call(f32[128,2048]{1,0:T(8,128)S(1)} %get-tuple-element.13.y_ref, f32[8,128]{1,0:T(8,128)S(1)} %bitcast.16), custom_call_target="tpu_custom_call" | custom-call | tf_op jit(solution)/shard_map/pallas_call | solution.py:182
Async XLA Ops:
  2.9 17.5 %copy-start.1 = (bf16[128,128]{1,0:T(8,128)(2,1)S(1)}, bf16[128,128]{1,0:T(8,128)(2,1)}, u32[]{:S(2)}) copy-start(bf16[128,128]{1,0:T(8,128)(2,1)} %c_ref.3) | copy-start | bytes 98308
  2.9 17.5 %copy-start.2 = (bf16[128,128]{1,0:T(8,128)(2,1)S(1)}, bf16[128,128]{1,0:T(8,128)(2,1)}, u32[]{:S(2)}) copy-start(bf16[128,128]{1,0:T(8,128)(2,1)} %b_hbm.1) | copy-start | bytes 98308
  2.9 17.5 %copy-start.3 = (f32[128,32]{0,1:T(8,128)S(1)}, f32[128,32]{0,1:T(8,128)}, u32[]{:S(2)}) copy-start(f32[128,32]{0,1:T(8,128)} %param.10) | copy-start | bytes 49156
  3.0 17.5 %copy-start.6 = (f32[32]{0:T(128)S(1)}, f32[32]{0:T(128)}, u32[]{:S(2)}) copy-start(f32[32]{0:T(128)} %param.11) | copy-start | bytes 388
  3.0 43.9 %all-to-all-start = ((f32[64,33,1,128]{3,2,1,0:T(1,128)}), f32[64,33,1,128]{3,2,1,0:T(1,128)S(1)}, u32[]{:S(2)}, u32[]{:S(2)}) async-start(f32[64,33,1,128]{3,2,1,0:T(1,128)} %bitcast.3), calls=%async_computation | async-start | bytes 2162688 | tf_op jit(solution)/shard_map/all_to_all | solution.py:190
  20.4 1.0 %copy-start = (bf16[128,2048]{1,0:T(8,128)(2,1)S(1)}, bf16[128,2048]{1,0:T(8,128)(2,1)}, u32[]{:S(2)}) copy-start(bf16[128,2048]{1,0:T(8,128)(2,1)} %x_hbm.1) | copy-start | bytes 1572868
  21.5 1.0 %copy-start.5 = (bf16[32,64,128]{2,1,0:T(8,128)(2,1)S(1)}, bf16[32,64,128]{2,1,0:T(8,128)(2,1)}, u32[]{:S(2)}) copy-start(bf16[32,64,128]{2,1,0:T(8,128)(2,1)} %init_ref.1) | copy-start | bytes 1572868
  47.0 31.7 %copy-start.4 = (f32[2048]{0:T(1024)S(1)}, f32[2048]{0:T(1024)}, u32[]{:S(2)}) copy-start(f32[2048]{0:T(1024)} %param.13) | copy-start | bytes 24580
